TPU v7x, 512 devices: a whole 4x4x16 slice. The times are simulated.
512 devices in a mesh: pair: 32 (over y, z_lo, core), mom: 16 (over x, z_hi).
Axes of the slice: x: 4, y: 4, z: 16 (z_hi: 4, z_lo: 4; z = z_hi * 4 + z_lo), core: 2. Of those that a mesh axis runs over, the one named last changes fastest.
Arguments:
- coefficients: bfloat16 [2048, 32768], P(None, 'pair'), may hold values from -0.0625 to 0.0625
- exponent: float32 [32768], P('pair'), may hold values from 0.5 to 8
- amplitude: float32 [32768], P('pair'), may hold values from 1 to 6
- centers: float32 [3, 32768], P(None, 'pair'), may hold values from -8 to 8
- momenta: float32 [3, 3072], P(None, 'mom'), may hold values from -2.5 to 2.5
- quad_weight: float32 [3072], P('mom'), may hold values from 0.25 to 4
Outputs:
- gram_matrix: float32 [2, 2048, 2048], P(None, 'pair', 'mom')
All inputs are finite; a program needn't handle non-finite values.
Results may differ from a plain program's by a relative error of at most 0.0028.
Values may be sent and summed in bfloat16 or wider, within the bound.
A program may use at most 64 MiB of HBM per device.

v0:
```python
import jax
import jax.numpy as jnp
from jax import lax
from jax.sharding import PartitionSpec as P


def make_integrals(exponent, amplitude, centers, momenta, quad_weight, count_all):
    squared = momenta[0] * momenta[0] + momenta[1] * momenta[1] + momenta[2] * momenta[2]
    phases = (
        centers[0][:, None] * momenta[0][None, :]
        + centers[1][:, None] * momenta[1][None, :]
        + centers[2][:, None] * momenta[2][None, :]
    )
    weight_root = jnp.sqrt(quad_weight / (count_all * (0.5 * squared + 0.5)))
    envelope = (
        amplitude[:, None]
        * jnp.exp(-squared[None, :] / (4.0 * exponent[:, None]))
        * weight_root[None, :]
    )
    return jnp.concatenate(
        [envelope * jnp.cos(phases), -envelope * jnp.sin(phases)], axis=1
    ).astype(jnp.bfloat16)


def gram_block(left_rows, right_rows):
    half_width = right_rows.shape[1] // 2
    swapped = jnp.concatenate([right_rows[:, half_width:], -right_rows[:, :half_width]], axis=1)
    dims = (((1,), (1,)), ((), ()))
    real_part = lax.dot_general(left_rows, right_rows, dims, preferred_element_type=jnp.float32)
    imag_part = lax.dot_general(left_rows, swapped, dims, preferred_element_type=jnp.float32)
    return jnp.stack([real_part, imag_part])


def per_device(coefficients, exponent, amplitude, centers, momenta, quad_weight):
    count_all = float(momenta.shape[1] * lax.axis_size("mom"))
    integ = make_integrals(exponent, amplitude, centers, momenta, quad_weight, count_all)
    own_rows = coefficients.shape[0] // lax.axis_size("pair")
    partial_sum = jnp.dot(coefficients, integ, preferred_element_type=jnp.float32)
    summed = lax.psum(partial_sum, "pair")
    rounded = summed.astype(jnp.bfloat16)
    own_block = lax.dynamic_slice_in_dim(rounded, lax.axis_index("pair") * own_rows, own_rows, 0)
    partials = gram_block(own_block, rounded)
    return lax.psum_scatter(partials, "mom", scatter_dimension=2, tiled=True)


def solution(mesh):
    return jax.shard_map(
        per_device,
        mesh=mesh,
        in_specs=(P(None, "pair"), P("pair"), P("pair"), P(None, "pair"), P(None, "mom"), P("mom")),
        out_specs=P(None, "pair", "mom"),
        check_vma=False,
    )
```

profile of v0, /device:TPU:16, one launch (start us, length us, event | category | flops | bytes accessed | tf_op | source)
XLA Modules:
  0.0 309.1 jit_solution(9644198573272633232)
XLA Ops:
  6.5 0.0 reduce-scatter.2.cloned.1.call-start
  6.5 0.8 add_negate_fusion
  7.3 0.8 fusion.16
  8.2 0.7 broadcast_multiply_fusion
  8.9 0.7 fusion.10
  9.6 4.2 %multiply_convert_fusion.1 = (bf16[1024,192]{0,1:T(8,128)(2,1)S(1)}, bf16[1024,192]{0,1:T(8,128)(2,1)S(1)}) fusion(f32[192]{0:T(256)S(1)} %bitcast.18, f32[1024]{0:T(1024)S(1)} %bitcast.22, f32[192]{0:T(256)S(1)} %bitcast.20, f32[1024]{0:T(1024)S(1)} %bitcast.23, f32[192]{0:T(256)S(1)} %bitcast.16, f32[1024]{0:T(1024)S(1)} %bitcast.21, f32[192]{0:T(256)S(1)} %fusion.10, ...), kind=kLoop, calls=%fused_computation.15 | loop fusion | flops 2555904 | bytes 810752 | tf_op jit(solution)/shard_map/convert
  13.7 5.7 %convolution_bitcast_fusion = f32[2048,384]{0,1:T(8,128)} fusion(bf16[2048,1024]{1,0:T(8,128)(2,1)} %param.6, bf16[1024,192]{0,1:T(8,128)(2,1)S(1)} %get-tuple-element.8, bf16[1024,192]{0,1:T(8,128)(2,1)S(1)} %get-tuple-element.7), kind=kOutput, calls=%fused_computation | convolution fusion | flops 1612185600 | bytes 8126464 | tf_op jit(solution)/shard_map/dot_general | solution.py:38
  19.4 145.4 %all-reduce.1 = bf16[2048,384]{0,1:T(8,128)(2,1)S(1)} all-reduce(f32[2048,384]{0,1:T(8,128)} %convolution_bitcast_fusion), channel_id=1, replica_groups=mesh['pair'=32,'mom'=16] {'pair'}, use_global_device_ids=true, to_apply=%region_0.0 | all-reduce | flops 786432 | bytes 4718592 | tf_op jit(solution)/shard_map/psum | solution.py:39
  164.9 0.1 fusion.15
  165.0 0.5 convolution_bitcast_fusion.2
  165.5 0.5 convolution_bitcast_fusion.1
  166.0 1.1 pad_maximum_fusion
  167.0 0.0 reduce-scatter.2.cloned.1.call-update
  167.1 135.2 %reduce-scatter.2.cloned.1.call-done = f32[2,64,128]{2,1,0:T(8,128)} async-done(((f32[2,64,2048]{2,1,0:T(8,128)}), f32[2,64,128]{2,1,0:T(8,128)}) %reduce-scatter.2.cloned.1.call-update) | async-done | bytes 65552 | tf_op jit(solution)/shard_map/reduce_scatter | solution.py:43
Async XLA Ops:
  6.5 295.7 %reduce-scatter.2.cloned.1.call-start = ((), (), s32[]{:S(2)}) async-start(), calls=%async_computation.1 | async-start | bytes 1114112 | tf_op jit(solution)/shard_map/reduce_scatter | solution.py:43
Sparse Core Ops, SparseCore 0:
  167.2 135.0 reduce-scatter.1
where the time goes:
time: 310 us; the launch traced here: 309 us
  blocking collectives  145 us (47%)
  waiting for transfers between devices  135 us (44%)
  between operations  13.4 us (4%)
  other arithmetic  7.52 us (2%)
  matrix products  6.64 us (2%)
    psum x1, blocking collectives, per_device(): summed = lax.psum(partial_sum, 'pair')  145 us
    reduce_scatter x1, waiting for transfers between devices, per_device(): return lax.psum_scatter(partials, 'mom', scatter_dimension=2, tiled=True)  135 us
  transfers between devices with their start and end apart: 1, of which 1 were waited for; matrix products, arithmetic and copies ran while one was open for 0% of the time, Pallas kernels for 0%

commit v1 on v0

v1 whole, which is shorter than its diff:
```python
import math

import jax
import jax.numpy as jnp
from jax import lax
from jax.experimental import pallas as pl
from jax.experimental.pallas import tpu as pltpu
from jax.sharding import PartitionSpec as P

MESH = pl.DeviceIdType.MESH
BF16, F32 = jnp.bfloat16, jnp.float32
NT = (((1,), (1,)), ((), ()))

RING = (2, 1, 3)


def _fit(values, degree):
    import numpy as np

    nodes = 0.125 * (1.0 - np.cos(np.pi * (np.arange(400) + 0.5) / 400))
    weights = np.polynomial.chebyshev.chebfit(8.0 * nodes - 1.0, values(nodes), degree)
    series = np.polynomial.Chebyshev(weights, domain=[0.0, 0.25])
    return [float(c) for c in series.convert(kind=np.polynomial.Polynomial).coef]


def _sin_over(v):
    import numpy as np

    u = np.sqrt(v)
    return 2.0 * np.sin(np.pi * u) / u


def _cos_of(v):
    import numpy as np

    return np.cos(np.pi * np.sqrt(v))


SIN_C = _fit(_sin_over, 4)
COS_C = _fit(_cos_of, 5)


def horner(coefs, v):
    total = coefs[-1] * v + coefs[-2]
    for c in coefs[-3::-1]:
        total = total * v + c
    return total


def encode(x):
    return (x * jnp.abs(x)).astype(BF16)


def decode(y):
    y = y.astype(F32)
    return y * lax.rsqrt(jnp.maximum(jnp.abs(y), 1e-37))


def kernel(
    coef_h, expo_h, amp_h, cen_h, mom_h, qw_h, out,
    coef_v, expo_v, amp_v, cen_v, mom_v, qw_v, rows_v, cols_v, integ,
    prod, core_s, core_r, y_s, y_own, y_r, z_s, z_r, r_own, b_all, a_all,
    x_s, x_own, x_r, g_s, g_r,
    in_sem, coef_sem, s1, s2, s3,
    core_ss, core_rs, y_ss, y_rs, z_ss, z_rs, yb_ss, yb_rs, cb_ss, cb_rs, za_ss, za_rs,
    x_ss, x_rs, g_ss, g_rs,
):
    pair, mom = lax.axis_index("pair"), lax.axis_index("mom")
    y, zl, c = pair // 8, (pair // 2) % 4, pair % 2
    x, zh = mom // 4, mom % 4
    z = zh * 4 + zl

    def dev(y=y, zl=zl, c=c, x=x, zh=zh):
        return {"pair": y * 8 + zl * 2 + c, "mom": x * 4 + zh}

    def at_z(step):
        far = (z + step + 16) % 16
        return dev(zl=far % 4, zh=far // 4)

    def send(src, dst, ss, rs, to):
        copy = pltpu.make_async_remote_copy(
            src_ref=src, dst_ref=dst, send_sem=ss, recv_sem=rs, device_id=to, device_id_type=MESH
        )
        copy.start()
        return copy

    small = [
        pltpu.make_async_copy(h, v, in_sem.at[i])
        for i, (h, v) in enumerate(
            [(expo_h, expo_v), (amp_h, amp_v), (cen_h, cen_v), (mom_h, mom_v), (qw_h, qw_v)]
        )
    ]
    for copy in small:
        copy.start()
    coef_in = []
    for t in range(4):
        copy = pltpu.make_async_copy(coef_h.at[:, (zl + 1 + t) % 4], coef_v.at[t], coef_sem.at[t])
        copy.start()
        coef_in.append(copy)

    barrier = pltpu.get_barrier_semaphore()
    near = [dev(c=1 - c)]
    near += [dev(y=(y + d) % 4) for d in RING]
    near += [dev(zl=(zl + d) % 4) for d in (1, 2, 3)]
    near += [dev(x=(x + d) % 4) for d in RING]
    near += [at_z(1), at_z(-1)]
    for to in near:
        pl.semaphore_signal(barrier, inc=1, device_id=to, device_id_type=MESH)

    for copy in small:
        copy.wait()
    m = mom_v[...]
    squared = m[0:1] * m[0:1] + m[1:2] * m[1:2] + m[2:3] * m[2:3]
    rows_v[...] = jnp.zeros_like(rows_v)
    rows_v[0:3, 0:192] = m
    rows_v[3:4, 0:192] = squared
    rows_v[4:5, 0:192] = jnp.sqrt(qw_v[...] / (3072.0 * (0.5 * squared + 0.5)))
    cols_v[...] = jnp.transpose(rows_v[...])
    cen_v[...] = cen_v[...] * (0.5 / math.pi)
    expo_v[...] = (-0.25 / math.log(2.0)) / expo_v[...]

    def integrals(i, carry):
        base = pl.multiple_of(i * 16, 16)
        k = cols_v[pl.ds(base, 16), :]
        turns = cen_v[0:1] * k[:, 0:1] + cen_v[1:2] * k[:, 1:2] + cen_v[2:3] * k[:, 2:3]
        u = turns - jnp.floor(turns + 0.5)
        v = u * u
        s = horner(SIN_C, v) * u
        envelope = (amp_v[...] * jnp.exp2(k[:, 3:4] * expo_v[...])) * k[:, 4:5]
        cosine = envelope - (0.5 * envelope) * (s * s)
        sine = (envelope * s) * horner(COS_C, v)
        first = i < 8
        row_c = pl.multiple_of(jnp.where(first, base, base + 128), 16)
        row_s = pl.multiple_of(jnp.where(first, base + 128, base + 192), 16)
        integ[pl.ds(row_c, 16), :] = cosine.astype(BF16)
        integ[pl.ds(row_s, 16), :] = (-sine).astype(BF16)
        return carry

    lax.fori_loop(0, 12, integrals, 0)

    core_c, y_c, z_c = [], [], []

    def contract(t):
        coef_in[t].wait()
        prod[t] = lax.dot_general(
            coef_v[t].reshape(512, 1024), integ[...], NT, preferred_element_type=F32
        ).reshape(4, 2, 64, 384)
        core_s[t] = encode(prod[t, :, 1 - c])
        if t == 0:
            pl.semaphore_wait(barrier, len(near))
        core_c.append(send(core_s.at[t], core_r.at[t], core_ss.at[t], core_rs.at[t], dev(c=1 - c)))

    def spread(t):
        core_c[t].wait_recv()
        total = prod[t, :, c] + decode(core_r[t])
        y_s[t] = encode(total)
        prod[t, :, c] = total
        y_own[t] = prod[t, y, c]
        y_c.append(
            [
                send(y_s.at[t, (y + d) % 4], y_r.at[t, i], y_ss.at[t, i], y_rs.at[t, i], dev(y=(y + d) % 4))
                for i, d in enumerate(RING)
            ]
        )

    contract(0)
    contract(1)
    for t in range(4):
        spread(t)
        if t < 2:
            contract(t + 2)
        if t == 1:
            for step in (1, -1):
                pl.semaphore_signal(s1, inc=1, device_id=at_z(step), device_id_type=MESH)

    for t in range(4):
        for copy in y_c[t]:
            copy.wait_recv()
        total = y_own[t]
        for i in range(3):
            total = total + decode(y_r[t, i])
        if t < 3:
            z_s[t] = encode(total)
            z_c.append(send(z_s.at[t], z_r.at[t], z_ss.at[t], z_rs.at[t], dev(zl=(zl + 1 + t) % 4)))
        if t == 0:
            pl.semaphore_wait(s1, 2)
            for step in (2, -2):
                pl.semaphore_signal(s2, inc=1, device_id=at_z(step), device_id_type=MESH)
    for t in range(3):
        z_c[t].wait_recv()
        total = total + decode(z_r[t])
    r_own[...] = total.astype(BF16)

    yb = [
        send(r_own, b_all.at[y, c], yb_ss.at[i], yb_rs.at[i], dev(y=(y + d) % 4)) for i, d in enumerate((1, 3, 2))
    ]
    za = [
        send(r_own, a_all.at[zl], za_ss.at[i], za_rs.at[i], dev(zl=(zl + d) % 4)) for i, d in enumerate((1, 3, 2))
    ]
    cb = [send(r_own, b_all.at[y, c], cb_ss.at[0], cb_rs.at[0], dev(c=1 - c))]
    b_all[y, c] = r_own[...]
    a_all[zl] = r_own[...]
    pl.semaphore_wait(s2, 2)
    for step in (4, -4):
        pl.semaphore_signal(s3, inc=1, device_id=at_z(step), device_id_type=MESH)
    for i, d in enumerate((1, 3, 2)):
        yb[i].wait_recv()
        here = b_all.at[(y + 4 - d) % 4, c]
        cb.append(send(here, here, cb_ss.at[i + 1], cb_rs.at[i + 1], dev(c=1 - c)))
    for copy in cb:
        copy.wait_recv()

    lane = lax.broadcasted_iota(jnp.int32, (64, 128), 1)
    sign = jnp.where(lane < 64, -1.0, 1.0).astype(F32)
    x_c, g_c = [], []
    for i, d in enumerate((0, 1, 3, 2)):
        r = (zl + 4 - d) % 4
        if d:
            za[i - 1].wait_recv()
        rows = a_all[r].astype(F32)
        turned = jnp.concatenate(
            [-rows[:, 128:256], rows[:, 0:128], pltpu.roll(rows[:, 256:384], 64, 1) * sign], axis=1
        )
        left = (jnp.concatenate([rows, turned], axis=0) * 2.0**32).astype(BF16)
        for n in range(4):
            block = lax.dot_general(left, b_all[n].reshape(128, 384), NT, preferred_element_type=F32)
            x_own[i, n] = block
            x_s[i, n] = encode(block)
        x_c.append(
            [
                send(x_s.at[i, (x + e) % 4], x_r.at[i, j], x_ss.at[i, j], x_rs.at[i, j], dev(x=(x + e) % 4))
                for j, e in enumerate(RING)
            ]
        )

    pl.semaphore_wait(s3, 2)
    for i, d in enumerate((0, 1, 3, 2)):
        r = (zl + 4 - d) % 4
        for copy in x_c[i]:
            copy.wait_recv()
        total = x_own[i, x]
        for j in range(3):
            total = total + decode(x_r[i, j])
        g_s[i] = encode(total)
        here = jnp.logical_and(r == zl, zh == zl)

        @pl.when(here)
        def _():
            g_r[zh] = g_s[i]

        @pl.when(jnp.logical_not(here))
        def _():
            send(g_s.at[i], g_r.at[zh], g_ss.at[i], g_rs.at[zh], dev(zl=r, zh=zl))

    total = jnp.zeros((128, 128), F32)
    for a in range(4):
        here = jnp.logical_and(zl == zh, zh == a)

        @pl.when(jnp.logical_not(here))
        def _():
            pltpu.make_async_remote_copy(
                src_ref=g_s.at[0], dst_ref=g_r.at[a], send_sem=g_ss.at[0], recv_sem=g_rs.at[a],
                device_id=dev(zl=zh, zh=a), device_id_type=MESH,
            ).wait_recv()

        total = total + decode(g_r[a])
    out[...] = (total * (2.0**-32)).reshape(2, 64, 128)

    for copy in core_c + [k for group in y_c for k in group] + z_c + yb + za + cb + [k for group in x_c for k in group]:
        copy.wait_send()
    for i, d in enumerate((0, 1, 3, 2)):
        r = (zl + 4 - d) % 4

        @pl.when(jnp.logical_not(jnp.logical_and(r == zl, zh == zl)))
        def _():
            pltpu.make_async_remote_copy(
                src_ref=g_s.at[i], dst_ref=g_r.at[0], send_sem=g_ss.at[i], recv_sem=g_rs.at[0],
                device_id=dev(zl=r, zh=zl), device_id_type=MESH,
            ).wait_send()


def per_device(coefficients, exponent, amplitude, centers, momenta, quad_weight):
    vmem, dma = pltpu.VMEM, pltpu.SemaphoreType.DMA
    regular = pltpu.SemaphoreType.REGULAR
    return pl.pallas_call(
        kernel,
        out_shape=jax.ShapeDtypeStruct((2, 64, 128), F32),
        in_specs=[pl.BlockSpec(memory_space=pl.ANY)] * 6,
        out_specs=pl.BlockSpec(memory_space=pltpu.VMEM),
        scratch_shapes=[
            vmem((4, 4, 128, 1024), BF16), vmem((1, 1024), F32), vmem((1, 1024), F32), vmem((3, 1024), F32),
            vmem((3, 192), F32), vmem((1, 192), F32), vmem((8, 256), F32), vmem((256, 8), F32),
            vmem((384, 1024), BF16),
            vmem((4, 4, 2, 64, 384), F32), vmem((4, 4, 64, 384), BF16), vmem((4, 4, 64, 384), BF16),
            vmem((4, 4, 64, 384), BF16), vmem((4, 64, 384), F32), vmem((4, 3, 64, 384), BF16),
            vmem((3, 64, 384), BF16), vmem((3, 64, 384), BF16), vmem((64, 384), BF16),
            vmem((4, 2, 64, 384), BF16), vmem((4, 64, 384), BF16),
            vmem((4, 4, 128, 128), BF16), vmem((4, 4, 128, 128), F32), vmem((4, 3, 128, 128), BF16),
            vmem((4, 128, 128), BF16), vmem((4, 128, 128), BF16),
            dma((5,)), dma((4,)), regular, regular, regular,
            dma((4,)), dma((4,)), dma((4, 3)), dma((4, 3)), dma((3,)), dma((3,)),
            dma((3,)), dma((3,)), dma((4,)), dma((4,)), dma((3,)), dma((3,)),
            dma((4, 3)), dma((4, 3)), dma((4,)), dma((4,)),
        ],
        compiler_params=pltpu.CompilerParams(
            collective_id=0, has_side_effects=True, vmem_limit_bytes=48 * 1024 * 1024
        ),
        name="scattering",
    )(
        coefficients.reshape(4, 4, 128, 1024),
        exponent.reshape(1, 1024),
        amplitude.reshape(1, 1024),
        centers,
        momenta,
        quad_weight.reshape(1, 192),
    )


def solution(mesh):
    return jax.shard_map(
        per_device,
        mesh=mesh,
        in_specs=(P(None, "pair"), P("pair"), P("pair"), P(None, "pair"), P(None, "mom"), P("mom")),
        out_specs=P(None, "pair", "mom"),
        check_vma=False,
    )
```

time: 310 us -> 58.3 us (0.19)
  the two profiles are of different devices: /device:TPU:16 before, /device:TPU:1 now
where the time goes in v1:
time: 58.3 us; the launch traced here: 58 us
  Pallas kernels  51.7 us (89%)
  local copies, waits for them, and re-layouts  6.27 us (11%)
    pallas_call x1, Pallas kernels, per_device(): pl.pallas_call(kernel, out_shape=jax.ShapeDtypeStruct((2, 64, 128), F32),...  51.7 us
    unnamed x13, local copies, waits for them, and re-layouts  6.27 us

profile of v1, /device:TPU:1, one launch (start us, length us, event | category | flops | bytes accessed | tf_op | source)
XLA Modules:
  0.0 58.0 jit_solution(7544557625467290905)
XLA Ops:
  0.0 0.0 copy-start
  0.0 2.2 %copy-done = bf16[2048,1024]{1,0:T(8,128)(2,1)S(1)} copy-done((bf16[2048,1024]{1,0:T(8,128)(2,1)S(1)}, bf16[2048,1024]{1,0:T(8,128)(2,1)}, u32[]{:S(2)}) %copy-start) | copy-done | bytes 4194328
  2.2 0.0 copy-start.1
  2.2 0.7 %copy-done.1 = f32[3,1024]{1,0:T(4,128)S(1)} copy-done((f32[3,1024]{1,0:T(4,128)S(1)}, f32[3,1024]{1,0:T(4,128)}, u32[]{:S(2)}) %copy-start.1) | copy-done | bytes 12312
  2.9 0.0 copy-start.2
  2.9 0.7 %copy-done.2 = f32[1024]{0:T(1024)S(1)} copy-done((f32[1024]{0:T(1024)S(1)}, f32[1024]{0:T(1024)}, u32[]{:S(2)}) %copy-start.2) | copy-done | bytes 4120
  3.6 0.0 copy-start.3
  3.6 0.7 %copy-done.3 = f32[1024]{0:T(1024)S(1)} copy-done((f32[1024]{0:T(1024)S(1)}, f32[1024]{0:T(1024)}, u32[]{:S(2)}) %copy-start.3) | copy-done | bytes 4120
  4.3 0.0 copy-start.4
  4.3 0.7 %copy-done.4 = f32[3,192]{1,0:T(4,128)S(1)} copy-done((f32[3,192]{1,0:T(4,128)S(1)}, f32[3,192]{1,0:T(4,128)}, u32[]{:S(2)}) %copy-start.4) | copy-done | bytes 2328
  5.0 0.0 copy-start.5
  5.0 0.7 %copy-done.5 = f32[192]{0:T(256)S(1)} copy-done((f32[192]{0:T(256)S(1)}, f32[192]{0:T(256)}, u32[]{:S(2)}) %copy-start.5) | copy-done | bytes 792
  5.6 51.7 %scattering.1 = f32[2,64,128]{2,1,0:T(8,128)S(1)} custom-call(bf16[4,4,128,1024]{3,2,1,0:T(8,128)(2,1)S(1)} %bitcast.4, f32[1,1024]{1,0:T(1,128)S(1)} %bitcast.5, f32[1,1024]{1,0:T(1,128)S(1)} %bitcast.6, f32[3,1024]{1,0:T(4,128)S(1)} %copy-done.1, f32[3,192]{1,0:T(4,128)S(1)} %copy-done.4, f32[1,192]{1,0:T(1,128)S(1)} %bitcast.7), custom_call_target="tpu_custom_call" | custom-call | tf_op jit(solution)/shard_map/scattering/pallas_call | solution.py:285
  57.4 0.6 %copy.8 = f32[2,64,128]{2,1,0:T(8,128)} copy(f32[2,64,128]{2,1,0:T(8,128)S(1)} %scattering.1) | data formatting | bytes 131072
Async XLA Ops:
  0.0 2.2 %copy-start = (bf16[2048,1024]{1,0:T(8,128)(2,1)S(1)}, bf16[2048,1024]{1,0:T(8,128)(2,1)}, u32[]{:S(2)}) copy-start(bf16[2048,1024]{1,0:T(8,128)(2,1)} %param.6) | copy-start | bytes 12582916
  2.2 0.7 %copy-start.1 = (f32[3,1024]{1,0:T(4,128)S(1)}, f32[3,1024]{1,0:T(4,128)}, u32[]{:S(2)}) copy-start(f32[3,1024]{1,0:T(4,128)} %cen_h.1) | copy-start | bytes 36868
  2.9 0.7 %copy-start.2 = (f32[1024]{0:T(1024)S(1)}, f32[1024]{0:T(1024)}, u32[]{:S(2)}) copy-start(f32[1024]{0:T(1024)} %param.7) | copy-start | bytes 12292
  3.6 0.7 %copy-start.3 = (f32[1024]{0:T(1024)S(1)}, f32[1024]{0:T(1024)}, u32[]{:S(2)}) copy-start(f32[1024]{0:T(1024)} %param.8) | copy-start | bytes 12292
  4.3 0.7 %copy-start.4 = (f32[3,192]{1,0:T(4,128)S(1)}, f32[3,192]{1,0:T(4,128)}, u32[]{:S(2)}) copy-start(f32[3,192]{1,0:T(4,128)} %mom_h.1) | copy-start | bytes 6916
  5.0 0.7 %copy-start.5 = (f32[192]{0:T(256)S(1)}, f32[192]{0:T(256)}, u32[]{:S(2)}) copy-start(f32[192]{0:T(256)} %param.11) | copy-start | bytes 2308

commit v2 on v1

--- a/solution.py
+++ b/solution.py
@@ -8,10 +8,12 @@
 from jax.sharding import PartitionSpec as P
 
 MESH = pl.DeviceIdType.MESH
+scope = jax.named_scope
 BF16, F32 = jnp.bfloat16, jnp.float32
 NT = (((1,), (1,)), ((), ()))
 
 RING = (2, 1, 3)
+LINE = (1, 3, 2, 0)
 
 
 def _fit(values, degree):
@@ -59,7 +61,7 @@
 def kernel(
     coef_h, expo_h, amp_h, cen_h, mom_h, qw_h, out,
     coef_v, expo_v, amp_v, cen_v, mom_v, qw_v, rows_v, cols_v, integ,
-    prod, core_s, core_r, y_s, y_own, y_r, z_s, z_r, r_own, b_all, a_all,
+    prod, core_s, core_r, y_s, y_r, z_s, z_r, r_own, b_all, a_all,
     x_s, x_own, x_r, g_s, g_r,
     in_sem, coef_sem, s1, s2, s3,
     core_ss, core_rs, y_ss, y_rs, z_ss, z_rs, yb_ss, yb_rs, cb_ss, cb_rs, za_ss, za_rs,
@@ -70,6 +72,16 @@
     x, zh = mom // 4, mom % 4
     z = zh * 4 + zl
 
+    def label(zl):
+        step = 3 - 3 * zl + 5 * (zl * (zl - 1) // 2) - 8 * (zl * (zl - 1) * (zl - 2) // 6)
+        return (zh + step) % 4
+
+    def holder(group, window):
+        o = (group - window + 4) % 4
+        return 1 + 2 * o - 3 * (o * (o - 1) // 2) + 2 * (o * (o - 1) * (o - 2) // 6)
+
+    group = label(zl)
+
     def dev(y=y, zl=zl, c=c, x=x, zh=zh):
         return {"pair": y * 8 + zl * 2 + c, "mom": x * 4 + zh}
 
@@ -94,7 +106,7 @@
         copy.start()
     coef_in = []
     for t in range(4):
-        copy = pltpu.make_async_copy(coef_h.at[:, (zl + 1 + t) % 4], coef_v.at[t], coef_sem.at[t])
+        copy = pltpu.make_async_copy(coef_h.at[:, label((zl + LINE[t]) % 4)], coef_v.at[t], coef_sem.at[t])
         copy.start()
         coef_in.append(copy)
 
@@ -107,8 +119,9 @@
     for to in near:
         pl.semaphore_signal(barrier, inc=1, device_id=to, device_id_type=MESH)
 
-    for copy in small:
-        copy.wait()
+    with scope("small_wait"):
+        for copy in small:
+            copy.wait()
     m = mom_v[...]
     squared = m[0:1] * m[0:1] + m[1:2] * m[1:2] + m[2:3] * m[2:3]
     rows_v[...] = jnp.zeros_like(rows_v)
@@ -136,26 +149,31 @@
         integ[pl.ds(row_s, 16), :] = (-sine).astype(BF16)
         return carry
 
-    lax.fori_loop(0, 12, integrals, 0)
+    with scope("integrals"):
+        lax.fori_loop(0, 12, integrals, 0)
 
     core_c, y_c, z_c = [], [], []
 
+    def half(t, core):
+        rows = coef_v[t, :, core].reshape(256, 1024)
+        return lax.dot_general(rows, integ[...], NT, preferred_element_type=F32).reshape(4, 64, 384)
+
     def contract(t):
-        coef_in[t].wait()
-        prod[t] = lax.dot_general(
-            coef_v[t].reshape(512, 1024), integ[...], NT, preferred_element_type=F32
-        ).reshape(4, 2, 64, 384)
-        core_s[t] = encode(prod[t, :, 1 - c])
+        with scope(f"coef_wait{t}"):
+            coef_in[t].wait()
+        core_s[t] = encode(half(t, 1 - c))
         if t == 0:
-            pl.semaphore_wait(barrier, len(near))
+            with scope("barrier"):
+                pl.semaphore_wait(barrier, len(near))
         core_c.append(send(core_s.at[t], core_r.at[t], core_ss.at[t], core_rs.at[t], dev(c=1 - c)))
+        prod[t] = half(t, c)
 
     def spread(t):
-        core_c[t].wait_recv()
-        total = prod[t, :, c] + decode(core_r[t])
+        with scope(f"core_wait{t}"):
+            core_c[t].wait_recv()
+        total = prod[t] + decode(core_r[t])
         y_s[t] = encode(total)
-        prod[t, :, c] = total
-        y_own[t] = prod[t, y, c]
+        prod[t] = total
         y_c.append(
             [
                 send(y_s.at[t, (y + d) % 4], y_r.at[t, i], y_ss.at[t, i], y_rs.at[t, i], dev(y=(y + d) % 4))
@@ -174,20 +192,22 @@
                 pl.semaphore_signal(s1, inc=1, device_id=at_z(step), device_id_type=MESH)
 
     for t in range(4):
-        for copy in y_c[t]:
-            copy.wait_recv()
-        total = y_own[t]
+        with scope(f"y_wait{t}"):
+            for copy in y_c[t]:
+                copy.wait_recv()
+        total = prod[t, y]
         for i in range(3):
             total = total + decode(y_r[t, i])
         if t < 3:
             z_s[t] = encode(total)
-            z_c.append(send(z_s.at[t], z_r.at[t], z_ss.at[t], z_rs.at[t], dev(zl=(zl + 1 + t) % 4)))
+            z_c.append(send(z_s.at[t], z_r.at[t], z_ss.at[t], z_rs.at[t], dev(zl=(zl + LINE[t]) % 4)))
         if t == 0:
             pl.semaphore_wait(s1, 2)
             for step in (2, -2):
                 pl.semaphore_signal(s2, inc=1, device_id=at_z(step), device_id_type=MESH)
     for t in range(3):
-        z_c[t].wait_recv()
+        with scope(f"z_wait{t}"):
+            z_c[t].wait_recv()
         total = total + decode(z_r[t])
     r_own[...] = total.astype(BF16)
 
@@ -195,28 +215,31 @@
         send(r_own, b_all.at[y, c], yb_ss.at[i], yb_rs.at[i], dev(y=(y + d) % 4)) for i, d in enumerate((1, 3, 2))
     ]
     za = [
-        send(r_own, a_all.at[zl], za_ss.at[i], za_rs.at[i], dev(zl=(zl + d) % 4)) for i, d in enumerate((1, 3, 2))
+        send(r_own, a_all.at[group], za_ss.at[i], za_rs.at[i], dev(zl=(zl + d) % 4)) for i, d in enumerate((1, 3, 2))
     ]
     cb = [send(r_own, b_all.at[y, c], cb_ss.at[0], cb_rs.at[0], dev(c=1 - c))]
     b_all[y, c] = r_own[...]
-    a_all[zl] = r_own[...]
+    a_all[group] = r_own[...]
     pl.semaphore_wait(s2, 2)
     for step in (4, -4):
         pl.semaphore_signal(s3, inc=1, device_id=at_z(step), device_id_type=MESH)
     for i, d in enumerate((1, 3, 2)):
-        yb[i].wait_recv()
+        with scope(f"yb_wait{i}"):
+            yb[i].wait_recv()
         here = b_all.at[(y + 4 - d) % 4, c]
         cb.append(send(here, here, cb_ss.at[i + 1], cb_rs.at[i + 1], dev(c=1 - c)))
-    for copy in cb:
-        copy.wait_recv()
+    with scope("cb_wait"):
+        for copy in cb:
+            copy.wait_recv()
 
     lane = lax.broadcasted_iota(jnp.int32, (64, 128), 1)
     sign = jnp.where(lane < 64, -1.0, 1.0).astype(F32)
     x_c, g_c = [], []
     for i, d in enumerate((0, 1, 3, 2)):
-        r = (zl + 4 - d) % 4
+        r = label((zl + 4 - d) % 4)
         if d:
-            za[i - 1].wait_recv()
+            with scope(f"za_wait{i}"):
+                za[i - 1].wait_recv()
         rows = a_all[r].astype(F32)
         turned = jnp.concatenate(
             [-rows[:, 128:256], rows[:, 0:128], pltpu.roll(rows[:, 256:384], 64, 1) * sign], axis=1
@@ -233,16 +256,18 @@
             ]
         )
 
-    pl.semaphore_wait(s3, 2)
+    with scope("s3_wait"):
+        pl.semaphore_wait(s3, 2)
     for i, d in enumerate((0, 1, 3, 2)):
-        r = (zl + 4 - d) % 4
-        for copy in x_c[i]:
-            copy.wait_recv()
+        r = label((zl + 4 - d) % 4)
+        with scope(f"x_wait{i}"):
+            for copy in x_c[i]:
+                copy.wait_recv()
         total = x_own[i, x]
         for j in range(3):
             total = total + decode(x_r[i, j])
         g_s[i] = encode(total)
-        here = jnp.logical_and(r == zl, zh == zl)
+        here = jnp.logical_and(r == zl, zh == group)
 
         @pl.when(here)
         def _():
@@ -250,18 +275,20 @@
 
         @pl.when(jnp.logical_not(here))
         def _():
-            send(g_s.at[i], g_r.at[zh], g_ss.at[i], g_rs.at[zh], dev(zl=r, zh=zl))
+            send(g_s.at[i], g_r.at[zh], g_ss.at[i], g_rs.at[zh], dev(zl=r, zh=group))
 
     total = jnp.zeros((128, 128), F32)
     for a in range(4):
-        here = jnp.logical_and(zl == zh, zh == a)
+        source = holder(zh, a)
+        here = jnp.logical_and(source == zl, zh == a)
 
         @pl.when(jnp.logical_not(here))
         def _():
-            pltpu.make_async_remote_copy(
-                src_ref=g_s.at[0], dst_ref=g_r.at[a], send_sem=g_ss.at[0], recv_sem=g_rs.at[a],
-                device_id=dev(zl=zh, zh=a), device_id_type=MESH,
-            ).wait_recv()
+            with scope(f"g_wait{a}"):
+                pltpu.make_async_remote_copy(
+                    src_ref=g_s.at[0], dst_ref=g_r.at[a], send_sem=g_ss.at[0], recv_sem=g_rs.at[a],
+                    device_id=dev(zl=source, zh=a), device_id_type=MESH,
+                ).wait_recv()
 
         total = total + decode(g_r[a])
     out[...] = (total * (2.0**-32)).reshape(2, 64, 128)
@@ -269,13 +296,13 @@
     for copy in core_c + [k for group in y_c for k in group] + z_c + yb + za + cb + [k for group in x_c for k in group]:
         copy.wait_send()
     for i, d in enumerate((0, 1, 3, 2)):
-        r = (zl + 4 - d) % 4
-
-        @pl.when(jnp.logical_not(jnp.logical_and(r == zl, zh == zl)))
+        r = label((zl + 4 - d) % 4)
+
+        @pl.when(jnp.logical_not(jnp.logical_and(r == zl, zh == group)))
         def _():
             pltpu.make_async_remote_copy(
                 src_ref=g_s.at[i], dst_ref=g_r.at[0], send_sem=g_ss.at[i], recv_sem=g_rs.at[0],
-                device_id=dev(zl=r, zh=zl), device_id_type=MESH,
+                device_id=dev(zl=r, zh=group), device_id_type=MESH,
             ).wait_send()
 
 
@@ -288,11 +315,11 @@
         in_specs=[pl.BlockSpec(memory_space=pl.ANY)] * 6,
         out_specs=pl.BlockSpec(memory_space=pltpu.VMEM),
         scratch_shapes=[
-            vmem((4, 4, 128, 1024), BF16), vmem((1, 1024), F32), vmem((1, 1024), F32), vmem((3, 1024), F32),
+            vmem((4, 4, 2, 64, 1024), BF16), vmem((1, 1024), F32), vmem((1, 1024), F32), vmem((3, 1024), F32),
             vmem((3, 192), F32), vmem((1, 192), F32), vmem((8, 256), F32), vmem((256, 8), F32),
             vmem((384, 1024), BF16),
-            vmem((4, 4, 2, 64, 384), F32), vmem((4, 4, 64, 384), BF16), vmem((4, 4, 64, 384), BF16),
-            vmem((4, 4, 64, 384), BF16), vmem((4, 64, 384), F32), vmem((4, 3, 64, 384), BF16),
+            vmem((4, 4, 64, 384), F32), vmem((4, 4, 64, 384), BF16), vmem((4, 4, 64, 384), BF16),
+            vmem((4, 4, 64, 384), BF16), vmem((4, 3, 64, 384), BF16),
             vmem((3, 64, 384), BF16), vmem((3, 64, 384), BF16), vmem((64, 384), BF16),
             vmem((4, 2, 64, 384), BF16), vmem((4, 64, 384), BF16),
             vmem((4, 4, 128, 128), BF16), vmem((4, 4, 128, 128), F32), vmem((4, 3, 128, 128), BF16),
@@ -303,11 +330,11 @@
             dma((4, 3)), dma((4, 3)), dma((4,)), dma((4,)),
         ],
         compiler_params=pltpu.CompilerParams(
-            collective_id=0, has_side_effects=True, vmem_limit_bytes=48 * 1024 * 1024
+            collective_id=0, has_side_effects=True, vmem_limit_bytes=60 * 1024 * 1024
         ),
         name="scattering",
     )(
-        coefficients.reshape(4, 4, 128, 1024),
+        coefficients.reshape(4, 4, 2, 64, 1024),
         exponent.reshape(1, 1024),
         amplitude.reshape(1, 1024),
         centers,

time: 58.3 us -> 53.4 us (0.916)
  the two profiles are of different devices: /device:TPU:1 before, /device:TPU:33 now
where the time goes in v2:
time: 53.4 us; the launch traced here: 53.2 us
  Pallas kernels  51.7 us (97%)
  local copies, waits for them, and re-layouts  1.47 us (3%)
    pallas_call x1, Pallas kernels, per_device(): pl.pallas_call(kernel, out_shape=jax.ShapeDtypeStruct((2, 64, 128), F32),...  51.7 us
    unnamed x1, local copies, waits for them, and re-layouts  1.47 us

profile of v2, /device:TPU:33, one launch (start us, length us, event | category | flops | bytes accessed | tf_op | source)
XLA Modules:
  0.0 53.2 jit_solution(2710607876487884544)
XLA Ops:
  0.0 51.7 %scattering.1 = f32[2,64,128]{2,1,0:T(8,128)} custom-call(bf16[4,4,2,64,1024]{4,3,2,1,0:T(8,128)(2,1)} %bitcast.4, f32[1,1024]{1,0:T(1,128)} %bitcast.5, f32[1,1024]{1,0:T(1,128)} %bitcast.6, f32[3,1024]{1,0:T(4,128)} %cen_h.1, f32[3,192]{1,0:T(4,128)} %mom_h.1, f32[1,192]{1,0:T(1,128)} %bitcast.7), custom_call_target="tpu_custom_call" | custom-call | tf_op jit(solution)/shard_map/scattering/pallas_call | solution.py:312
  51.7 1.5 %copy.8 = f32[2,64,128]{2,1,0:T(8,128)} copy(f32[2,64,128]{2,1,0:T(8,128)} %scattering.1) | data formatting | bytes 131072

commit v3 on v2

v3 whole, which is shorter than its diff:
```python
import math

import jax
import jax.numpy as jnp
from jax import lax
from jax.experimental import pallas as pl
from jax.experimental.pallas import tpu as pltpu
from jax.sharding import PartitionSpec as P

MESH = pl.DeviceIdType.MESH
scope = jax.named_scope
BF16, F32 = jnp.bfloat16, jnp.float32
NT = (((1,), (1,)), ((), ()))

RING = (2, 1, 3)
NEAR = (1, 3, 2)
LINE = (2, 1, 3, 0)


def _fit(values, degree):
    import numpy as np

    nodes = 0.125 * (1.0 - np.cos(np.pi * (np.arange(400) + 0.5) / 400))
    weights = np.polynomial.chebyshev.chebfit(8.0 * nodes - 1.0, values(nodes), degree)
    series = np.polynomial.Chebyshev(weights, domain=[0.0, 0.25])
    return [float(c) for c in series.convert(kind=np.polynomial.Polynomial).coef]


def _sin_over(v):
    import numpy as np

    u = np.sqrt(v)
    return 2.0 * np.sin(np.pi * u) / u


def _cos_of(v):
    import numpy as np

    return np.cos(np.pi * np.sqrt(v))


SIN_C = _fit(_sin_over, 4)
COS_C = _fit(_cos_of, 5)


def horner(coefs, v):
    total = coefs[-1] * v + coefs[-2]
    for c in coefs[-3::-1]:
        total = total * v + c
    return total


def encode(x):
    return (x * jnp.abs(x)).astype(BF16)


def decode(y):
    y = y.astype(F32)
    return y * lax.rsqrt(jnp.maximum(jnp.abs(y), 1e-37))


def kernel(
    coef_h, expo_h, amp_h, cen_h, mom_h, qw_h, out,
    coef_v, expo_v, amp_v, cen_v, mom_v, qw_v, rows_v, cols_v, integ,
    prod, core_s, core_r, y_s, y_r, z_s, z_r, r_own, b_all, a_all,
    x_s, x_own, x_r, g_s, g_r,
    in_sem, coef_sem, s1, s2, s3,
    core_ss, core_rs, y_ss, y_rs, z_ss, z_rs, ca_ss, ca_rs, yb_ss, yb_rs, za_ss, za_rs,
    x_ss, x_rs, g_ss, g_rs,
):
    pair, mom = lax.axis_index("pair"), lax.axis_index("mom")
    y, zl, c = pair // 8, (pair // 2) % 4, pair % 2
    x, zh = mom // 4, mom % 4
    z = zh * 4 + zl

    def label(zl):
        step = 3 - zl - zl * (zl - 1) // 2 + 4 * (zl * (zl - 1) * (zl - 2) // 6)
        return (zh + step) % 4

    def holder(group, window):
        o = (group - window + 4) % 4
        return 2 + o - 3 * (o * (o - 1) // 2) + 4 * (o * (o - 1) * (o - 2) // 6)

    group = label(zl)

    def dev(y=y, zl=zl, c=c, x=x, zh=zh):
        return {"pair": y * 8 + zl * 2 + c, "mom": x * 4 + zh}

    def at_z(step, c=c):
        far = (z + step + 16) % 16
        return dev(zl=far % 4, c=c, zh=far // 4)

    def send(src, dst, ss, rs, to):
        copy = pltpu.make_async_remote_copy(
            src_ref=src, dst_ref=dst, send_sem=ss, recv_sem=rs, device_id=to, device_id_type=MESH
        )
        copy.start()
        return copy

    small = [
        pltpu.make_async_copy(h, v, in_sem.at[i])
        for i, (h, v) in enumerate(
            [(expo_h, expo_v), (amp_h, amp_v), (cen_h, cen_v), (mom_h, mom_v), (qw_h, qw_v)]
        )
    ]
    for copy in small:
        copy.start()
    barrier = pltpu.get_barrier_semaphore()
    near = [dev(c=1 - c)]
    near += [dev(y=(y + d) % 4) for d in RING]
    near += [dev(zl=(zl + d) % 4) for d in (1, 2, 3)]
    near += [dev(x=(x + d) % 4) for d in RING]
    near += [at_z(1), at_z(-1), at_z(1, 1 - c), at_z(-1, 1 - c)]
    for to in near:
        pl.semaphore_signal(barrier, inc=1, device_id=to, device_id_type=MESH)

    with scope("small_wait"):
        for copy in small:
            copy.wait()
    coef_in = []
    for t in range(4):
        copy = pltpu.make_async_copy(coef_h.at[:, label((zl + LINE[t]) % 4)], coef_v.at[t], coef_sem.at[t])
        copy.start()
        coef_in.append(copy)
    m = mom_v[...]
    squared = m[0:1] * m[0:1] + m[1:2] * m[1:2] + m[2:3] * m[2:3]
    rows_v[...] = jnp.zeros_like(rows_v)
    rows_v[0:3, 0:192] = m
    rows_v[3:4, 0:192] = squared
    rows_v[4:5, 0:192] = jnp.sqrt(qw_v[...] / (3072.0 * (0.5 * squared + 0.5)))
    cols_v[...] = jnp.transpose(rows_v[...])
    cen_v[...] = cen_v[...] * (0.5 / math.pi)
    expo_v[...] = (-0.25 / math.log(2.0)) / expo_v[...]

    def integrals(i, carry):
        base = pl.multiple_of(i * 16, 16)
        k = cols_v[pl.ds(base, 16), :]
        first = i < 8
        row_c = pl.multiple_of(jnp.where(first, base, base + 128), 16)
        row_s = pl.multiple_of(jnp.where(first, base + 128, base + 192), 16)
        for start in range(0, 1024, 256):
            p = slice(start, start + 256)
            turns = cen_v[0:1, p] * k[:, 0:1] + cen_v[1:2, p] * k[:, 1:2] + cen_v[2:3, p] * k[:, 2:3]
            u = turns - jnp.round(turns)
            v = u * u
            s = horner(SIN_C, v) * u
            envelope = (amp_v[:, p] * jnp.exp2(k[:, 3:4] * expo_v[:, p])) * k[:, 4:5]
            integ[pl.ds(row_c, 16), p] = (envelope - (0.5 * envelope) * (s * s)).astype(BF16)
            integ[pl.ds(row_s, 16), p] = (-((envelope * s) * horner(COS_C, v))).astype(BF16)
        return carry

    with scope("integrals"):
        lax.fori_loop(0, 12, integrals, 0, unroll=12)

    core_c, y_c, z_c = [], [], []

    def half(t, core):
        rows = coef_v[t, :, core].reshape(256, 1024)
        return lax.dot_general(rows, integ[...], NT, preferred_element_type=F32).reshape(4, 64, 384)

    def contract(t):
        with scope(f"coef_wait{t}"):
            coef_in[t].wait()
        core_s[t] = encode(half(t, 1 - c))
        if t == 0:
            with scope("barrier"):
                pl.semaphore_wait(barrier, len(near))
        core_c.append(send(core_s.at[t], core_r.at[t], core_ss.at[t], core_rs.at[t], dev(c=1 - c)))
        prod[t] = half(t, c)

    def spread(t):
        with scope(f"core_wait{t}"):
            core_c[t].wait_recv()
        total = prod[t] + decode(core_r[t])
        prod[t] = total
        y_s[t] = encode(total)
        y_c.append(
            [
                send(y_s.at[t, (y + d) % 4], y_r.at[t, i], y_ss.at[t, i], y_rs.at[t, i], dev(y=(y + d) % 4))
                for i, d in enumerate(RING)
            ]
        )

    contract(0)
    contract(1)
    for t in range(4):
        spread(t)
        if t < 2:
            contract(t + 2)
        if t == 1:
            for step in (1, -1):
                pl.semaphore_signal(s1, inc=1, device_id=at_z(step), device_id_type=MESH)

    for t in range(4):
        with scope(f"y_wait{t}"):
            for copy in y_c[t]:
                copy.wait_recv()
        total = prod[t, y]
        for i in range(3):
            total = total + decode(y_r[t, i])
        if t < 3:
            z_s[t] = encode(total)
            z_c.append(send(z_s.at[t], z_r.at[t], z_ss.at[t], z_rs.at[t], dev(zl=(zl + LINE[t]) % 4)))
        if t == 0:
            pl.semaphore_wait(s1, 2)
            for step in (2, -2):
                pl.semaphore_signal(s2, inc=1, device_id=at_z(step), device_id_type=MESH)
    for t in range(3):
        with scope(f"z_wait{t}"):
            z_c[t].wait_recv()
        total = total + decode(z_r[t])
    r_own[...] = (total * 65536.0).astype(BF16)

    ca = [send(r_own, a_all.at[group, c], ca_ss.at[0], ca_rs.at[0], dev(c=1 - c))]
    yb = [
        send(r_own, b_all.at[y, 0], yb_ss.at[i], yb_rs.at[i], dev(y=(y + d) % 4)) for i, d in enumerate(NEAR)
    ]
    za = [
        send(r_own, a_all.at[group, c], za_ss.at[i], za_rs.at[i], dev(zl=(zl + d) % 4)) for i, d in enumerate(NEAR)
    ]
    lane = lax.broadcasted_iota(jnp.int32, (64, 128), 1)

    def turn(n):
        rows = b_all[n, 0].astype(F32)
        last = pltpu.roll(rows[:, 256:384], 64, 1) * jnp.where(lane < 64, 1.0, -1.0)
        b_all[n, 1] = jnp.concatenate([rows[:, 128:256], -rows[:, 0:128], last], axis=1).astype(BF16)

    b_all[y, 0] = r_own[...]
    a_all[group, c] = r_own[...]
    pl.semaphore_wait(s2, 2)
    for step in (4, -4):
        pl.semaphore_signal(s3, inc=1, device_id=at_z(step), device_id_type=MESH)
    x_c = []
    with scope("ca_wait0"):
        ca[0].wait_recv()
    left = a_all[group].reshape(128, 384)
    def forward(i):
        with scope(f"za_wait{i}"):
            za[i].wait_recv()
        here = a_all.at[label((zl + 4 - NEAR[i]) % 4), c]
        ca.append(send(here, here, ca_ss.at[i + 1], ca_rs.at[i + 1], dev(c=1 - c)))

    for i, d in enumerate((0, *NEAR)):
        n = (y + 4 - d) % 4
        if i == 3:
            forward(0)
            forward(1)
        if d:
            with scope(f"yb_wait{i}"):
                yb[i - 1].wait_recv()
        turn(n)
        block = lax.dot_general(left, b_all[n].reshape(128, 384), NT, preferred_element_type=F32)
        x_own[0, n] = block
        x_s[0, n] = encode(block)
        e = (n - x + 4) % 4

        @pl.when(e > 0)
        def _():
            send(x_s.at[0, n], x_r.at[0, e - 1], x_ss.at[0, e - 1], x_rs.at[0, e - 1], dev(x=n))

    x_c.append(
        [
            pltpu.make_async_remote_copy(
                src_ref=x_s.at[0, 0], dst_ref=x_r.at[0, j], send_sem=x_ss.at[0, j], recv_sem=x_rs.at[0, j],
                device_id=dev(x=(x + 1) % 4), device_id_type=MESH,
            )
            for j in range(3)
        ]
    )

    def tile(i):
        with scope(f"ca_wait{i}"):
            ca[i].wait_recv()
        left = a_all[label((zl + 4 - (0, *NEAR)[i]) % 4)].reshape(128, 384)
        block = lax.dot_general(left, b_all[...].reshape(512, 384), NT, preferred_element_type=F32)
        for n in range(4):
            x_own[i, n] = block[:, n * 128 : n * 128 + 128]
            x_s[i, n] = encode(block[:, n * 128 : n * 128 + 128])
        x_c.append(
            [
                send(x_s.at[i, (x + e) % 4], x_r.at[i, j], x_ss.at[i, j], x_rs.at[i, j], dev(x=(x + e) % 4))
                for j, e in enumerate(RING)
            ]
        )

    forward(2)
    for i in range(1, 4):
        tile(i)

    with scope("s3_wait"):
        pl.semaphore_wait(s3, 2)
    for i in range(4):
        r = label((zl + 4 - (0, *NEAR)[i]) % 4)
        with scope(f"x_wait{i}"):
            for copy in x_c[i]:
                copy.wait_recv()
        total = x_own[i, x]
        for j in range(3):
            total = total + decode(x_r[i, j])
        g_s[i] = encode(total).reshape(2, 64, 128)
        for half in range(2):
            here = jnp.logical_and(jnp.logical_and(r == zl, zh == group), c == half)

            @pl.when(here)
            def _():
                g_r[zh, c] = g_s[i, half]

            @pl.when(jnp.logical_not(here))
            def _():
                send(
                    g_s.at[i, half], g_r.at[zh, c], g_ss.at[i, half], g_rs.at[zh, c],
                    dev(zl=r, c=half, zh=group),
                )

    with scope("left"):
        for copy in core_c + sum(y_c, []) + z_c + ca + yb + za + sum(x_c, []):
            copy.wait_send()

    total = [jnp.zeros((64, 128), F32)] * 2
    for a in range(4):
        source = holder(zh, a)
        for core in range(2):
            here = jnp.logical_and(jnp.logical_and(source == zl, zh == a), c == core)

            @pl.when(jnp.logical_not(here))
            def _():
                with scope(f"g_wait{a}{core}"):
                    pltpu.make_async_remote_copy(
                        src_ref=g_s.at[0, 0], dst_ref=g_r.at[a, core], send_sem=g_ss.at[0, 0],
                        recv_sem=g_rs.at[a, core], device_id=dev(zl=source, c=core, zh=a), device_id_type=MESH,
                    ).wait_recv()

            total[core] = total[core] + decode(g_r[a, core])
    first, second = total[0] * 2.0**-32, total[1] * 2.0**-32
    out[0] = jnp.where(lane < 64, first, pltpu.roll(second, 64, 1))
    out[1] = jnp.where(lane < 64, pltpu.roll(first, 64, 1), second)

    for i in range(4):
        r = label((zl + 4 - (0, *NEAR)[i]) % 4)
        for half in range(2):
            here = jnp.logical_and(jnp.logical_and(r == zl, zh == group), c == half)

            @pl.when(jnp.logical_not(here))
            def _():
                pltpu.make_async_remote_copy(
                    src_ref=g_s.at[i, half], dst_ref=g_r.at[0, 0], send_sem=g_ss.at[i, half], recv_sem=g_rs.at[0, 0],
                    device_id=dev(zl=r, c=half, zh=group), device_id_type=MESH,
                ).wait_send()


def per_device(coefficients, exponent, amplitude, centers, momenta, quad_weight):
    vmem, dma = pltpu.VMEM, pltpu.SemaphoreType.DMA
    regular = pltpu.SemaphoreType.REGULAR
    return pl.pallas_call(
        kernel,
        out_shape=pltpu.VMEM((2, 64, 128), F32),
        in_specs=[pl.BlockSpec(memory_space=pl.ANY)] * 6,
        out_specs=pl.BlockSpec(memory_space=pltpu.VMEM),
        scratch_shapes=[
            vmem((4, 4, 2, 64, 1024), BF16), vmem((1, 1024), F32), vmem((1, 1024), F32), vmem((3, 1024), F32),
            vmem((3, 192), F32), vmem((1, 192), F32), vmem((8, 256), F32), vmem((256, 8), F32),
            vmem((384, 1024), BF16),
            vmem((4, 4, 64, 384), F32), vmem((4, 4, 64, 384), BF16), vmem((4, 4, 64, 384), BF16),
            vmem((4, 4, 64, 384), BF16), vmem((4, 3, 64, 384), BF16),
            vmem((3, 64, 384), BF16), vmem((3, 64, 384), BF16), vmem((64, 384), BF16),
            vmem((4, 2, 64, 384), BF16), vmem((4, 2, 64, 384), BF16),
            vmem((4, 4, 128, 128), BF16), vmem((4, 4, 128, 128), F32), vmem((4, 3, 128, 128), BF16),
            vmem((4, 2, 64, 128), BF16), vmem((4, 2, 64, 128), BF16),
            dma((5,)), dma((4,)), regular, regular, regular,
            dma((4,)), dma((4,)), dma((4, 3)), dma((4, 3)), dma((3,)), dma((3,)),
            dma((4,)), dma((4,)), dma((3,)), dma((3,)), dma((3,)), dma((3,)),
            dma((4, 3)), dma((4, 3)), dma((4, 2)), dma((4, 2)),
        ],
        compiler_params=pltpu.CompilerParams(
            collective_id=0, has_side_effects=True, vmem_limit_bytes=60 * 1024 * 1024
        ),
        name="scattering",
    )(
        coefficients.reshape(4, 4, 2, 64, 1024),
        exponent.reshape(1, 1024),
        amplitude.reshape(1, 1024),
        centers,
        momenta,
        quad_weight.reshape(1, 192),
    )


def solution(mesh):
    return jax.shard_map(
        per_device,
        mesh=mesh,
        in_specs=(P(None, "pair"), P("pair"), P("pair"), P(None, "pair"), P(None, "mom"), P("mom")),
        out_specs=P(None, "pair", "mom"),
        check_vma=False,
    )
```

time: 53.4 us -> 48.3 us (0.904)
  the two profiles are of different devices: /device:TPU:33 before, /device:TPU:57 now
where the time goes in v3:
time: 48.3 us; the launch traced here: 48.1 us
  Pallas kernels  47.5 us (98%)
  local copies, waits for them, and re-layouts  0.63 us (1%)
    pallas_call x1, Pallas kernels, per_device(): pl.pallas_call(kernel, out_shape=pltpu.VMEM((2, 64, 128), F32), in_specs=...  47.5 us

profile of v3, /device:TPU:57, one launch (start us, length us, event | category | flops | bytes accessed | tf_op | source)
XLA Modules:
  0.0 48.1 jit_solution(6798151631685624595)
XLA Ops:
  0.0 47.5 %scattering.1 = f32[2,64,128]{2,1,0:T(8,128)S(1)} custom-call(bf16[4,4,2,64,1024]{4,3,2,1,0:T(8,128)(2,1)} %bitcast.4, f32[1,1024]{1,0:T(1,128)} %bitcast.5, f32[1,1024]{1,0:T(1,128)} %bitcast.6, f32[3,1024]{1,0:T(4,128)} %cen_h.1, f32[3,192]{1,0:T(4,128)} %mom_h.1, f32[1,192]{1,0:T(1,128)} %bitcast.7), custom_call_target="tpu_custom_call" | custom-call | tf_op jit(solution)/shard_map/scattering/pallas_call | solution.py:354
  47.5 0.6 %copy.8 = f32[2,64,128]{2,1,0:T(8,128)} copy(f32[2,64,128]{2,1,0:T(8,128)S(1)} %scattering.1) | data formatting | bytes 131072

commit v4 on v3

v4 whole, which is shorter than its diff:
```python
import math

import jax
import jax.numpy as jnp
from jax import lax
from jax.experimental import pallas as pl
from jax.experimental.pallas import tpu as pltpu
from jax.sharding import PartitionSpec as P

MESH = pl.DeviceIdType.MESH
scope = jax.named_scope
BF16, F32 = jnp.bfloat16, jnp.float32
NT = (((1,), (1,)), ((), ()))

RING = (2, 1, 3)
NEAR = (1, 3, 2)
LINE = (2, 1, 3, 0)


def _fit(values, degree):
    import numpy as np

    nodes = 0.125 * (1.0 - np.cos(np.pi * (np.arange(400) + 0.5) / 400))
    weights = np.polynomial.chebyshev.chebfit(8.0 * nodes - 1.0, values(nodes), degree)
    series = np.polynomial.Chebyshev(weights, domain=[0.0, 0.25])
    return [float(c) for c in series.convert(kind=np.polynomial.Polynomial).coef]


def _sin_over(v):
    import numpy as np

    u = np.sqrt(v)
    return 2.0 * np.sin(np.pi * u) / u


def _cos_of(v):
    import numpy as np

    return np.cos(np.pi * np.sqrt(v))


SIN_C = _fit(_sin_over, 4)
COS_C = _fit(_cos_of, 5)


def horner(coefs, v):
    total = coefs[-1] * v + coefs[-2]
    for c in coefs[-3::-1]:
        total = total * v + c
    return total


def encode(x):
    return (x * jnp.abs(x)).astype(BF16)


def decode(y):
    y = y.astype(F32)
    return y * lax.rsqrt(jnp.maximum(jnp.abs(y), 1e-37))


def kernel(
    coef_h, expo_h, amp_h, cen_h, mom_h, qw_h, out,
    coef_v, expo_v, amp_v, cen_v, mom_v, qw_v, rows_v, cols_v, integ,
    prod, core_s, core_r, y_s, y_r, z_s, z_r, r_own, b_all, a_all,
    x_s, x_own, x_r, g_s, g_r,
    in_sem, coef_sem, heard,
    core_ss, core_rs, y_ss, y_rs, z_ss, z_rs, ca_ss, ca_rs, yb_ss, yb_rs, za_ss, za_rs,
    x_ss, x_rs, g_ss, g_rs,
):
    pair, mom = lax.axis_index("pair"), lax.axis_index("mom")
    y, zl, c = pair // 8, (pair // 2) % 4, pair % 2
    x, zh = mom // 4, mom % 4
    z = zh * 4 + zl

    def label(zl):
        return (zl + 3 - 2 * (zh // 2)) % 4

    def holder(group, window):
        return (group + 1 + 2 * (window // 2)) % 4

    group = label(zl)

    def dev(y=y, zl=zl, c=c, x=x, zh=zh):
        return {"pair": y * 8 + zl * 2 + c, "mom": x * 4 + zh}

    def each_way(k, act):
        for step in (2**k, -(2**k)):
            far = z + step

            @pl.when(jnp.logical_and(far >= 0, far < 16))
            def _():
                act(far)

    def ways(k):
        return (z + 16 - 2**k) // 16 + (31 - z - 2**k) // 16

    def tell(k):
        def act(far):
            to = dev(zl=far % 4, zh=far // 4)
            pl.semaphore_signal(heard.at[k], inc=1, device_id=to, device_id_type=MESH)

        each_way(k, act)

    def hear(k):
        pl.semaphore_wait(heard.at[k], ways(k))

    def send(src, dst, ss, rs, to):
        copy = pltpu.make_async_remote_copy(
            src_ref=src, dst_ref=dst, send_sem=ss, recv_sem=rs, device_id=to, device_id_type=MESH
        )
        copy.start()
        return copy

    def bytes_of(ref, ss, rs):
        return pltpu.make_async_remote_copy(
            src_ref=ref, dst_ref=ref, send_sem=ss, recv_sem=rs, device_id=dev(c=1 - c), device_id_type=MESH
        )

    small = [
        pltpu.make_async_copy(h, v, in_sem.at[i])
        for i, (h, v) in enumerate(
            [(expo_h, expo_v), (amp_h, amp_v), (cen_h, cen_v), (mom_h, mom_v), (qw_h, qw_v)]
        )
    ]
    for copy in small:
        copy.start()
    barrier = pltpu.get_barrier_semaphore()
    near = [dev(c=1 - c)]
    near += [dev(y=(y + d) % 4) for d in RING]
    near += [dev(zl=(zl + d) % 4) for d in (1, 2, 3)]
    near += [dev(x=(x + d) % 4) for d in RING]
    for to in near:
        pl.semaphore_signal(barrier, inc=1, device_id=to, device_id_type=MESH)

    def greet(far):
        for core in range(2):
            to = dev(zl=far % 4, zh=far // 4, c=core)
            pl.semaphore_signal(barrier, inc=1, device_id=to, device_id_type=MESH)

    each_way(0, greet)
    greeted = len(near) + 2 * ways(0)

    with scope("small_wait"):
        for copy in small:
            copy.wait()
    coef_in = []
    for t in range(4):
        copy = pltpu.make_async_copy(coef_h.at[:, label((zl + LINE[t]) % 4)], coef_v.at[t], coef_sem.at[t])
        copy.start()
        coef_in.append(copy)
    m = mom_v[...]
    squared = m[0:1] * m[0:1] + m[1:2] * m[1:2] + m[2:3] * m[2:3]
    rows_v[...] = jnp.zeros_like(rows_v)
    rows_v[0:3, 0:192] = m
    rows_v[3:4, 0:192] = squared
    rows_v[4:5, 0:192] = jnp.sqrt(qw_v[...] / (3072.0 * (0.5 * squared + 0.5)))
    cols_v[...] = jnp.transpose(rows_v[...])
    cen_v[...] = cen_v[...] * (0.5 / math.pi)
    expo_v[...] = (-0.25 / math.log(2.0)) / expo_v[...]

    def integrals(i, carry):
        base = pl.multiple_of(i * 16, 16)
        k = cols_v[pl.ds(base, 16), :]
        first = i < 8
        row_c = pl.multiple_of(jnp.where(first, base, base + 128), 16)
        row_s = pl.multiple_of(jnp.where(first, base + 128, base + 192), 16)
        for start in range(0, 1024, 256):
            p = slice(start, start + 256)
            turns = cen_v[0:1, p] * k[:, 0:1] + cen_v[1:2, p] * k[:, 1:2] + cen_v[2:3, p] * k[:, 2:3]
            u = turns - jnp.round(turns)
            v = u * u
            s = horner(SIN_C, v) * u
            envelope = (amp_v[:, p] * jnp.exp2(k[:, 3:4] * expo_v[:, p])) * k[:, 4:5]
            integ[pl.ds(row_c, 16), p] = (envelope - (0.5 * envelope) * (s * s)).astype(BF16)
            integ[pl.ds(row_s, 16), p] = (-((envelope * s) * horner(COS_C, v))).astype(BF16)
        return carry

    with scope("integrals"):
        lax.fori_loop(0, 12, integrals, 0, unroll=12)


    def half(t, core):
        rows = coef_v[t, :, core].reshape(256, 1024)
        return lax.dot_general(rows, integ[...], NT, preferred_element_type=F32).reshape(4, 64, 384)

    def contract(t):
        with scope(f"coef_wait{t}"):
            coef_in[t].wait()
        core_s[t] = encode(half(t, 1 - c))
        if t == 0:
            with scope("barrier"):
                pl.semaphore_wait(barrier, greeted)
        send(core_s.at[t], core_r.at[t], core_ss, core_rs.at[t], dev(c=1 - c))
        prod[t] = half(t, c)

    def spread(t):
        with scope(f"core_wait{t}"):
            bytes_of(core_r.at[t], core_ss, core_rs.at[t]).wait_recv()
        total = prod[t] + decode(core_r[t])
        prod[t] = total
        y_s[t] = encode(total)
        for i, d in enumerate(RING):
            send(y_s.at[t, (y + d) % 4], y_r.at[t, i], y_ss, y_rs.at[t], dev(y=(y + d) % 4))

    contract(0)
    contract(1)
    for t in range(4):
        spread(t)
        if t < 2:
            contract(t + 2)
        if t == 1:
            tell(0)

    for t in range(4):
        with scope(f"y_wait{t}"):
            bytes_of(y_r.at[t], y_ss, y_rs.at[t]).wait_recv()
        total = prod[t, y]
        for i in range(3):
            total = total + decode(y_r[t, i])
        if t < 3:
            z_s[t] = encode(total)
            send(z_s.at[t], z_r.at[t], z_ss, z_rs, dev(zl=(zl + LINE[t]) % 4))
        if t in (0, 2):
            hear(t // 2)
            tell(t // 2 + 1)
    with scope("z_wait"):
        bytes_of(z_r, z_ss, z_rs).wait_recv()
    for t in range(3):
        total = total + decode(z_r[t])
    r_own[...] = (total * 65536.0).astype(BF16)

    ca = [send(r_own, a_all.at[group, c], ca_ss, ca_rs.at[0], dev(c=1 - c))]
    yb = [
        send(r_own, b_all.at[y, 0], yb_ss, yb_rs.at[i], dev(y=(y + d) % 4)) for i, d in enumerate(NEAR)
    ]
    za = [
        send(r_own, a_all.at[group, c], za_ss, za_rs.at[i], dev(zl=(zl + d) % 4)) for i, d in enumerate(NEAR)
    ]
    lane = lax.broadcasted_iota(jnp.int32, (64, 128), 1)

    def turn(n):
        rows = b_all[n, 0].astype(F32)
        last = pltpu.roll(rows[:, 256:384], 64, 1) * jnp.where(lane < 64, 1.0, -1.0)
        b_all[n, 1] = jnp.concatenate([rows[:, 128:256], -rows[:, 0:128], last], axis=1).astype(BF16)

    b_all[y, 0] = r_own[...]
    a_all[group, c] = r_own[...]
    hear(2)
    tell(3)
    x_c = []
    with scope("ca_wait0"):
        ca[0].wait_recv()
    left = a_all[group].reshape(128, 384)
    def forward(i):
        with scope(f"za_wait{i}"):
            za[i].wait_recv()
        here = a_all.at[label((zl + 4 - NEAR[i]) % 4), c]
        ca.append(send(here, here, ca_ss, ca_rs.at[i + 1], dev(c=1 - c)))

    for i, d in enumerate((0, *NEAR)):
        n = (y + 4 - d) % 4
        if d:
            with scope(f"yb_wait{i}"):
                yb[i - 1].wait_recv()
        turn(n)
        block = lax.dot_general(left, b_all[n].reshape(128, 384), NT, preferred_element_type=F32)
        x_own[0, n] = block.reshape(2, 64, 128)
        x_s[0, n] = encode(block).reshape(2, 64, 128)
        e = (n - x + 4) % 4

        @pl.when(e > 0)
        def _():
            send(x_s.at[0, n], x_r.at[0, e - 1], x_ss, x_rs.at[0], dev(x=n))

        if d:
            forward(i - 1)

    halves = [(i, half) for half in range(2) for i in range(1, 4)]
    for i, half in halves:
        core = (c + half) % 2
        if half:
            with scope(f"ca_wait{i}"):
                ca[i].wait_recv()
        left = a_all[label((zl + 4 - (0, *NEAR)[i]) % 4), core]
        block = lax.dot_general(left, b_all[...].reshape(512, 384), NT, preferred_element_type=F32)
        for n in range(4):
            x_own[i, n, core] = block[:, n * 128 : n * 128 + 128]
            x_s[i, n, core] = encode(block[:, n * 128 : n * 128 + 128])
        for j, e in enumerate(RING):
            n = (x + e) % 4
            send(x_s.at[i, n, core], x_r.at[i, j, core], x_ss, x_rs.at[i + 3 * half], dev(x=n))

    with scope("hear3"):
        hear(3)
    for k, (i, half) in enumerate([(0, 0), (0, 1), *halves]):
        r = label((zl + 4 - (0, *NEAR)[i]) % 4)
        core = (c + half) % 2
        if k != 1:
            with scope(f"x_wait{i}{half}"):
                landed = x_r.at[i, :, core] if i else x_r.at[0]
                bytes_of(landed, x_ss, x_rs.at[i + 3 * half]).wait_recv()
        total = x_own[i, x, core]
        for j in range(3):
            total = total + decode(x_r[i, j, core])
        g_s[i, core] = encode(total)
        to = (g_s.at[i, core], g_r.at[zh, c], g_ss.at[half], g_rs.at[zh], dev(zl=r, c=core, zh=group))
        if half:
            send(*to)
        else:
            here = jnp.logical_and(r == zl, zh == group)

            @pl.when(here)
            def _():
                g_r[zh, c] = g_s[i, core]

            @pl.when(jnp.logical_not(here))
            def _():
                send(*to)

    with scope("left"):
        for ref, sem in (
            (core_r, core_ss), (y_r, y_ss), (z_r, z_ss), (a_all.at[:, 0], ca_ss), (z_r, yb_ss), (z_r, za_ss), (x_r, x_ss)
        ):
            bytes_of(ref, sem, z_rs).wait_send()

    total = [jnp.zeros((64, 128), F32)] * 2
    for a in range(4):
        here = jnp.logical_and(holder(zh, a) == zl, zh == a)

        @pl.when(here)
        def _():
            bytes_of(g_r.at[a, 0], g_ss.at[0], g_rs.at[a]).wait_recv()

        @pl.when(jnp.logical_not(here))
        def _():
            with scope(f"g_wait{a}"):
                bytes_of(g_r.at[a], g_ss.at[0], g_rs.at[a]).wait_recv()

        for core in range(2):
            total[core] = total[core] + decode(g_r[a, core])
    first, second = total[0] * 2.0**-32, total[1] * 2.0**-32
    out[0] = jnp.where(lane < 64, first, pltpu.roll(second, 64, 1))
    out[1] = jnp.where(lane < 64, pltpu.roll(first, 64, 1), second)

    bytes_of(g_s.at[:, 0], g_ss.at[1], z_rs).wait_send()
    here = group == zh

    @pl.when(here)
    def _():
        bytes_of(g_s.at[0:3, 0], g_ss.at[0], z_rs).wait_send()

    @pl.when(jnp.logical_not(here))
    def _():
        bytes_of(g_s.at[:, 0], g_ss.at[0], z_rs).wait_send()


def per_device(coefficients, exponent, amplitude, centers, momenta, quad_weight):
    vmem, dma = pltpu.VMEM, pltpu.SemaphoreType.DMA
    return pl.pallas_call(
        kernel,
        out_shape=pltpu.VMEM((2, 64, 128), F32),
        in_specs=[pl.BlockSpec(memory_space=pl.ANY)] * 6,
        out_specs=pl.BlockSpec(memory_space=pltpu.VMEM),
        scratch_shapes=[
            vmem((4, 4, 2, 64, 1024), BF16), vmem((1, 1024), F32), vmem((1, 1024), F32), vmem((3, 1024), F32),
            vmem((3, 192), F32), vmem((1, 192), F32), vmem((8, 256), F32), vmem((256, 8), F32),
            vmem((384, 1024), BF16),
            vmem((4, 4, 64, 384), F32), vmem((4, 4, 64, 384), BF16), vmem((4, 4, 64, 384), BF16),
            vmem((4, 4, 64, 384), BF16), vmem((4, 3, 64, 384), BF16),
            vmem((3, 64, 384), BF16), vmem((3, 64, 384), BF16), vmem((64, 384), BF16),
            vmem((4, 2, 64, 384), BF16), vmem((4, 2, 64, 384), BF16),
            vmem((4, 4, 2, 64, 128), BF16), vmem((4, 4, 2, 64, 128), F32), vmem((4, 3, 2, 64, 128), BF16),
            vmem((4, 2, 64, 128), BF16), vmem((4, 2, 64, 128), BF16),
            dma((5,)), dma((4,)), pltpu.SemaphoreType.REGULAR((4,)),
            dma, dma((4,)), dma, dma((4,)), dma, dma, dma, dma((4,)), dma, dma((3,)), dma, dma((3,)),
            dma, dma((7,)), dma((2,)), dma((4,)),
        ],
        compiler_params=pltpu.CompilerParams(
            collective_id=0, has_side_effects=True, vmem_limit_bytes=60 * 1024 * 1024
        ),
        name="scattering",
    )(
        coefficients.reshape(4, 4, 2, 64, 1024),
        exponent.reshape(1, 1024),
        amplitude.reshape(1, 1024),
        centers,
        momenta,
        quad_weight.reshape(1, 192),
    )


def solution(mesh):
    return jax.shard_map(
        per_device,
        mesh=mesh,
        in_specs=(P(None, "pair"), P("pair"), P("pair"), P(None, "pair"), P(None, "mom"), P("mom")),
        out_specs=P(None, "pair", "mom"),
        check_vma=False,
    )
```

time: 48.3 us -> 47 us (0.973)
  the two profiles are of different devices: /device:TPU:57 before, /device:TPU:33 now
where the time goes in v4:
time: 47 us; the launch traced here: 46.8 us
  Pallas kernels  46.2 us (98%)
  local copies, waits for them, and re-layouts  0.63 us (1%)
    pallas_call x1, Pallas kernels, per_device(): pl.pallas_call(kernel, out_shape=pltpu.VMEM((2, 64, 128), F32), in_specs=...  46.2 us

profile of v4, /device:TPU:33, one launch (start us, length us, event | category | flops | bytes accessed | tf_op | source)
XLA Modules:
  0.0 46.8 jit_solution(18275536155794640910)
XLA Ops:
  0.0 46.2 %scattering.1 = f32[2,64,128]{2,1,0:T(8,128)S(1)} custom-call(bf16[4,4,2,64,1024]{4,3,2,1,0:T(8,128)(2,1)} %bitcast.4, f32[1,1024]{1,0:T(1,128)} %bitcast.5, f32[1,1024]{1,0:T(1,128)} %bitcast.6, f32[3,1024]{1,0:T(4,128)} %cen_h.1, f32[3,192]{1,0:T(4,128)} %mom_h.1, f32[1,192]{1,0:T(1,128)} %bitcast.7), custom_call_target="tpu_custom_call" | custom-call | tf_op jit(solution)/shard_map/scattering/pallas_call | solution.py:360
  46.2 0.6 %copy.8 = f32[2,64,128]{2,1,0:T(8,128)} copy(f32[2,64,128]{2,1,0:T(8,128)S(1)} %scattering.1) | data formatting | bytes 131072

commit v5 on v4

--- a/solution.py
+++ b/solution.py
@@ -14,6 +14,7 @@
 
 RING = (2, 1, 3)
 NEAR = (1, 3, 2)
+ALONG = (3, 2, 1)
 LINE = (2, 1, 3, 0)
 
 
@@ -191,6 +192,7 @@
         if t == 0:
             with scope("barrier"):
                 pl.semaphore_wait(barrier, greeted)
+            tell(0)
         send(core_s.at[t], core_r.at[t], core_ss, core_rs.at[t], dev(c=1 - c))
         prod[t] = half(t, c)
 
@@ -210,7 +212,11 @@
         if t < 2:
             contract(t + 2)
         if t == 1:
-            tell(0)
+            hear(0)
+            tell(1)
+        if t == 3:
+            hear(1)
+            tell(2)
 
     for t in range(4):
         with scope(f"y_wait{t}"):
@@ -221,9 +227,9 @@
         if t < 3:
             z_s[t] = encode(total)
             send(z_s.at[t], z_r.at[t], z_ss, z_rs, dev(zl=(zl + LINE[t]) % 4))
-        if t in (0, 2):
-            hear(t // 2)
-            tell(t // 2 + 1)
+        if t == 2:
+            hear(2)
+            tell(3)
     with scope("z_wait"):
         bytes_of(z_r, z_ss, z_rs).wait_recv()
     for t in range(3):
@@ -235,7 +241,7 @@
         send(r_own, b_all.at[y, 0], yb_ss, yb_rs.at[i], dev(y=(y + d) % 4)) for i, d in enumerate(NEAR)
     ]
     za = [
-        send(r_own, a_all.at[group, c], za_ss, za_rs.at[i], dev(zl=(zl + d) % 4)) for i, d in enumerate(NEAR)
+        send(r_own, a_all.at[group, c], za_ss, za_rs.at[i], dev(zl=(zl + d) % 4)) for i, d in enumerate(ALONG)
     ]
     lane = lax.broadcasted_iota(jnp.int32, (64, 128), 1)
 
@@ -246,8 +252,6 @@
 
     b_all[y, 0] = r_own[...]
     a_all[group, c] = r_own[...]
-    hear(2)
-    tell(3)
     x_c = []
     with scope("ca_wait0"):
         ca[0].wait_recv()
@@ -255,7 +259,7 @@
     def forward(i):
         with scope(f"za_wait{i}"):
             za[i].wait_recv()
-        here = a_all.at[label((zl + 4 - NEAR[i]) % 4), c]
+        here = a_all.at[label((zl + 4 - ALONG[i]) % 4), c]
         ca.append(send(here, here, ca_ss, ca_rs.at[i + 1], dev(c=1 - c)))
 
     for i, d in enumerate((0, *NEAR)):
@@ -282,7 +286,7 @@
         if half:
             with scope(f"ca_wait{i}"):
                 ca[i].wait_recv()
-        left = a_all[label((zl + 4 - (0, *NEAR)[i]) % 4), core]
+        left = a_all[label((zl + 4 - (0, *ALONG)[i]) % 4), core]
         block = lax.dot_general(left, b_all[...].reshape(512, 384), NT, preferred_element_type=F32)
         for n in range(4):
             x_own[i, n, core] = block[:, n * 128 : n * 128 + 128]
@@ -294,7 +298,7 @@
     with scope("hear3"):
         hear(3)
     for k, (i, half) in enumerate([(0, 0), (0, 1), *halves]):
-        r = label((zl + 4 - (0, *NEAR)[i]) % 4)
+        r = label((zl + 4 - (0, *ALONG)[i]) % 4)
         core = (c + half) % 2
         if k != 1:
             with scope(f"x_wait{i}{half}"):

time: 47 us -> 46.1 us (0.981)
  Pallas kernels: 46.2 us -> 45.3 us
    pallas_call x1, Pallas kernels: 46.2 us -> 45.3 us  [per_device(): pl.pallas_call(kernel, out_shape=pltpu.VMEM((2, 64, 128), F32), in_specs=...]
where the time goes in v5:
time: 46.1 us; the launch traced here: 45.9 us
  Pallas kernels  45.3 us (98%)
  local copies, waits for them, and re-layouts  0.63 us (1%)
    pallas_call x1, Pallas kernels, per_device(): pl.pallas_call(kernel, out_shape=pltpu.VMEM((2, 64, 128), F32), in_specs=...  45.3 us

profile of v5, /device:TPU:33, one launch (start us, length us, event | category | flops | bytes accessed | tf_op | source)
XLA Modules:
  0.0 45.9 jit_solution(16857397297627685809)
XLA Ops:
  0.0 45.3 %scattering.1 = f32[2,64,128]{2,1,0:T(8,128)S(1)} custom-call(bf16[4,4,2,64,1024]{4,3,2,1,0:T(8,128)(2,1)} %bitcast.4, f32[1,1024]{1,0:T(1,128)} %bitcast.5, f32[1,1024]{1,0:T(1,128)} %bitcast.6, f32[3,1024]{1,0:T(4,128)} %cen_h.1, f32[3,192]{1,0:T(4,128)} %mom_h.1, f32[1,192]{1,0:T(1,128)} %bitcast.7), custom_call_target="tpu_custom_call" | custom-call | tf_op jit(solution)/shard_map/scattering/pallas_call | solution.py:364
  45.3 0.6 %copy.8 = f32[2,64,128]{2,1,0:T(8,128)} copy(f32[2,64,128]{2,1,0:T(8,128)S(1)} %scattering.1) | data formatting | bytes 131072

commit v6 on v5

--- a/solution.py
+++ b/solution.py
@@ -14,6 +14,8 @@
 
 RING = (2, 1, 3)
 NEAR = (1, 3, 2)
+ALL, LOW, HIGH = pl.ds(0, 64), pl.ds(0, 32), pl.ds(32, 32)
+PARTS = ((ALL,), (ALL,), (LOW, HIGH), (ALL,))
 ALONG = (3, 2, 1)
 LINE = (2, 1, 3, 0)
 
@@ -31,17 +33,17 @@
     import numpy as np
 
     u = np.sqrt(v)
-    return 2.0 * np.sin(np.pi * u) / u
+    return math.sqrt(2.0) * np.sin(np.pi * u) / u
 
 
 def _cos_of(v):
     import numpy as np
 
-    return np.cos(np.pi * np.sqrt(v))
+    return -math.sqrt(2.0) * np.cos(np.pi * np.sqrt(v))
 
 
 SIN_C = _fit(_sin_over, 4)
-COS_C = _fit(_cos_of, 5)
+COS_C = _fit(_cos_of, 4)
 
 
 def horner(coefs, v):
@@ -173,8 +175,9 @@
             v = u * u
             s = horner(SIN_C, v) * u
             envelope = (amp_v[:, p] * jnp.exp2(k[:, 3:4] * expo_v[:, p])) * k[:, 4:5]
-            integ[pl.ds(row_c, 16), p] = (envelope - (0.5 * envelope) * (s * s)).astype(BF16)
-            integ[pl.ds(row_s, 16), p] = (-((envelope * s) * horner(COS_C, v))).astype(BF16)
+            product = envelope * s
+            integ[pl.ds(row_c, 16), p] = (envelope - product * s).astype(BF16)
+            integ[pl.ds(row_s, 16), p] = (product * horner(COS_C, v)).astype(BF16)
         return carry
 
     with scope("integrals"):
@@ -202,8 +205,10 @@
         total = prod[t] + decode(core_r[t])
         prod[t] = total
         y_s[t] = encode(total)
-        for i, d in enumerate(RING):
-            send(y_s.at[t, (y + d) % 4], y_r.at[t, i], y_ss, y_rs.at[t], dev(y=(y + d) % 4))
+        for k, rows in enumerate(PARTS[t]):
+            for i, d in enumerate(RING):
+                to = dev(y=(y + d) % 4)
+                send(y_s.at[t, (y + d) % 4, rows], y_r.at[t, i, rows], y_ss, y_rs.at[t + 4 * k], to)
 
     contract(0)
     contract(1)
@@ -219,17 +224,19 @@
             tell(2)
 
     for t in range(4):
-        with scope(f"y_wait{t}"):
-            bytes_of(y_r.at[t], y_ss, y_rs.at[t]).wait_recv()
-        total = prod[t, y]
-        for i in range(3):
-            total = total + decode(y_r[t, i])
-        if t < 3:
-            z_s[t] = encode(total)
-            send(z_s.at[t], z_r.at[t], z_ss, z_rs, dev(zl=(zl + LINE[t]) % 4))
+        for k, rows in enumerate(PARTS[t]):
+            with scope(f"y_wait{t}{k}"):
+                bytes_of(y_r.at[t, :, rows], y_ss, y_rs.at[t + 4 * k]).wait_recv()
+            total = prod[t, y, rows]
+            for i in range(3):
+                total = total + decode(y_r[t, i, rows])
+            if t < 3:
+                z_s[t, rows] = encode(total)
+                send(z_s.at[t, rows], z_r.at[t, rows], z_ss, z_rs, dev(zl=(zl + LINE[t]) % 4))
         if t == 2:
             hear(2)
             tell(3)
+
     with scope("z_wait"):
         bytes_of(z_r, z_ss, z_rs).wait_recv()
     for t in range(3):
@@ -377,7 +384,7 @@
             vmem((4, 4, 2, 64, 128), BF16), vmem((4, 4, 2, 64, 128), F32), vmem((4, 3, 2, 64, 128), BF16),
             vmem((4, 2, 64, 128), BF16), vmem((4, 2, 64, 128), BF16),
             dma((5,)), dma((4,)), pltpu.SemaphoreType.REGULAR((4,)),
-            dma, dma((4,)), dma, dma((4,)), dma, dma, dma, dma((4,)), dma, dma((3,)), dma, dma((3,)),
+            dma, dma((4,)), dma, dma((8,)), dma, dma, dma, dma((4,)), dma, dma((3,)), dma, dma((3,)),
             dma, dma((7,)), dma((2,)), dma((4,)),
         ],
         compiler_params=pltpu.CompilerParams(

time: 46.1 us -> 45.8 us (level)
  no operation moved by 1% of the time
where the time goes in v6:
time: 45.8 us; the launch traced here: 45.7 us
  Pallas kernels  45 us (98%)
  local copies, waits for them, and re-layouts  0.63 us (1%)
    pallas_call x1, Pallas kernels, per_device(): pl.pallas_call(kernel, out_shape=pltpu.VMEM((2, 64, 128), F32), in_specs=...  45 us

profile of v6, /device:TPU:33, one launch (start us, length us, event | category | flops | bytes accessed | tf_op | source)
XLA Modules:
  0.0 45.7 jit_solution(17418501962187595325)
XLA Ops:
  0.0 45.0 %scattering.1 = f32[2,64,128]{2,1,0:T(8,128)S(1)} custom-call(bf16[4,4,2,64,1024]{4,3,2,1,0:T(8,128)(2,1)} %bitcast.4, f32[1,1024]{1,0:T(1,128)} %bitcast.5, f32[1,1024]{1,0:T(1,128)} %bitcast.6, f32[3,1024]{1,0:T(4,128)} %cen_h.1, f32[3,192]{1,0:T(4,128)} %mom_h.1, f32[1,192]{1,0:T(1,128)} %bitcast.7), custom_call_target="tpu_custom_call" | custom-call | tf_op jit(solution)/shard_map/scattering/pallas_call | solution.py:371
  45.0 0.6 %copy.8 = f32[2,64,128]{2,1,0:T(8,128)} copy(f32[2,64,128]{2,1,0:T(8,128)S(1)} %scattering.1) | data formatting | bytes 131072

commit v7 on v6

--- a/solution.py
+++ b/solution.py
@@ -137,21 +137,23 @@
         pl.semaphore_signal(barrier, inc=1, device_id=to, device_id_type=MESH)
 
     def greet(far):
-        for core in range(2):
-            to = dev(zl=far % 4, zh=far // 4, c=core)
+        @pl.when(far // 4 != zh)
+        def _():
+            to = dev(zl=far % 4, zh=far // 4)
             pl.semaphore_signal(barrier, inc=1, device_id=to, device_id_type=MESH)
 
     each_way(0, greet)
-    greeted = len(near) + 2 * ways(0)
-
-    with scope("small_wait"):
-        for copy in small:
-            copy.wait()
+    greeted = len(near) + (3 - zl) // 3 * ((zh + 3) // 4) + zl // 3 * ((6 - zh) // 4)
+
     coef_in = []
     for t in range(4):
         copy = pltpu.make_async_copy(coef_h.at[:, label((zl + LINE[t]) % 4)], coef_v.at[t], coef_sem.at[t])
         copy.start()
         coef_in.append(copy)
+
+    with scope("small_wait"):
+        for copy in small:
+            copy.wait()
     m = mom_v[...]
     squared = m[0:1] * m[0:1] + m[1:2] * m[1:2] + m[2:3] * m[2:3]
     rows_v[...] = jnp.zeros_like(rows_v)
@@ -208,7 +210,7 @@
         for k, rows in enumerate(PARTS[t]):
             for i, d in enumerate(RING):
                 to = dev(y=(y + d) % 4)
-                send(y_s.at[t, (y + d) % 4, rows], y_r.at[t, i, rows], y_ss, y_rs.at[t + 4 * k], to)
+                send(y_s.at[t, (y + d) % 4, rows], y_r.at[t, i, rows], y_ss, y_rs.at[t + 2 * k], to)
 
     contract(0)
     contract(1)
@@ -226,7 +228,7 @@
     for t in range(4):
         for k, rows in enumerate(PARTS[t]):
             with scope(f"y_wait{t}{k}"):
-                bytes_of(y_r.at[t, :, rows], y_ss, y_rs.at[t + 4 * k]).wait_recv()
+                bytes_of(y_r.at[t, :, rows], y_ss, y_rs.at[t + 2 * k]).wait_recv()
             total = prod[t, y, rows]
             for i in range(3):
                 total = total + decode(y_r[t, i, rows])
@@ -384,7 +386,7 @@
             vmem((4, 4, 2, 64, 128), BF16), vmem((4, 4, 2, 64, 128), F32), vmem((4, 3, 2, 64, 128), BF16),
             vmem((4, 2, 64, 128), BF16), vmem((4, 2, 64, 128), BF16),
             dma((5,)), dma((4,)), pltpu.SemaphoreType.REGULAR((4,)),
-            dma, dma((4,)), dma, dma((8,)), dma, dma, dma, dma((4,)), dma, dma((3,)), dma, dma((3,)),
+            dma, dma((4,)), dma, dma((5,)), dma, dma, dma, dma((4,)), dma, dma((3,)), dma, dma((3,)),
             dma, dma((7,)), dma((2,)), dma((4,)),
         ],
         compiler_params=pltpu.CompilerParams(

time: 45.8 us -> 45.8 us (level)
  no operation moved by 1% of the time
where the time goes in v7:
time: 45.8 us; the launch traced here: 45.7 us
  Pallas kernels  45.1 us (98%)
  local copies, waits for them, and re-layouts  0.63 us (1%)
    pallas_call x1, Pallas kernels, per_device(): pl.pallas_call(kernel, out_shape=pltpu.VMEM((2, 64, 128), F32), in_specs=...  45.1 us

profile of v7, /device:TPU:33, one launch (start us, length us, event | category | flops | bytes accessed | tf_op | source)
XLA Modules:
  0.0 45.7 jit_solution(10044569374708859301)
XLA Ops:
  0.0 45.1 %scattering.1 = f32[2,64,128]{2,1,0:T(8,128)S(1)} custom-call(bf16[4,4,2,64,1024]{4,3,2,1,0:T(8,128)(2,1)} %bitcast.4, f32[1,1024]{1,0:T(1,128)} %bitcast.5, f32[1,1024]{1,0:T(1,128)} %bitcast.6, f32[3,1024]{1,0:T(4,128)} %cen_h.1, f32[3,192]{1,0:T(4,128)} %mom_h.1, f32[1,192]{1,0:T(1,128)} %bitcast.7), custom_call_target="tpu_custom_call" | custom-call | tf_op jit(solution)/shard_map/scattering/pallas_call | solution.py:373
  45.1 0.6 %copy.8 = f32[2,64,128]{2,1,0:T(8,128)} copy(f32[2,64,128]{2,1,0:T(8,128)S(1)} %scattering.1) | data formatting | bytes 131072
